TPU v7x, 128 devices: a whole 4x4x4 slice. The times are simulated.
128 devices in a mesh: grp: 4 (over x_lo, core), seq: 32 (over z, x_hi, y).
Axes of the slice: x: 4 (x_hi: 2, x_lo: 2; x = x_hi * 2 + x_lo), y: 4, z: 4, core: 2. Of those that a mesh axis runs over, the one named last changes fastest.
Arguments:
- branch_query: bfloat16 [128, 128, 4096], P(('grp', 'seq')), may hold values from -36 to 36
- branch_key: bfloat16 [128, 128, 512], P(('grp', 'seq')), may hold values from -36 to 36
- branch_value_rows: bfloat16 [128, 128, 512], P(('grp', 'seq')), may hold values from -6 to 6
- prefix_key_rows: bfloat16 [8192, 512], P(('grp', 'seq')), may hold values from -6 to 6
- prefix_value_rows: bfloat16 [8192, 512], P(('grp', 'seq')), may hold values from -6 to 6
- grad_out: bfloat16 [128, 128, 4096], P(('grp', 'seq')), may hold values from -6 to 6
- branch_length: int32 [128], P(('grp', 'seq')), may hold values from 64 to 128
- branch_prefix: int32 [128], P(('grp', 'seq')), may hold values from 0 to 3
- replay_count: int32 [128], P(('grp', 'seq')), may hold values from 1 to 16
Outputs:
- grad_query: bfloat16 [128, 128, 4096], P(('grp', 'seq'))
- grad_branch_key: bfloat16 [128, 128, 512], P(('grp', 'seq'))
- grad_branch_value: bfloat16 [128, 128, 512], P(('grp', 'seq'))
- grad_prefix_key: bfloat16 [8192, 512], P(('grp', 'seq'))
All inputs are finite; a program needn't handle non-finite values.
Results may differ from a plain program's by a relative error of at most 0.013.
Values may be sent and summed in bfloat16 or wider, within the bound.
A program may use at most 128 MiB of HBM per device.

v0:
```python
import functools
import math

import jax
import jax.numpy as jnp
from jax import lax
from jax.experimental import pallas as pl
from jax.experimental.pallas import tpu as pltpu
from jax.sharding import PartitionSpec as P

f32, bf16 = jnp.float32, jnp.bfloat16
MESH = pl.DeviceIdType.MESH
SCALE = 1.0 / math.sqrt(128.0)
EXP2_SCALE = math.log2(math.e) / math.sqrt(128.0)
NEG = -1e30
HALVES = (("y", "z"), ("z", "y"))
HEADS, BRANCHES, KV = 2, 2, 2


def dot(a, b, ca, cb):
    return lax.dot_general(a, b, (((ca,), (cb,)), ((), ())), preferred_element_type=f32)


def place():
    g, s = lax.axis_index("grp"), lax.axis_index("seq")
    return dict(x=((s // 4) % 2) * 2 + g // 2, y=s % 4, z=s // 8, core=g % 2)


def device(at):
    return ((at["x"] % 2) * 2 + at["core"], at["z"] * 8 + (at["x"] // 2) * 4 + at["y"])


def peer(at, axis, distance, other_core=0):
    to = dict(at)
    if axis is not None:
        to[axis] = (at[axis] + distance) % 4
    if other_core:
        to["core"] = 1 - at["core"]
    return device(to)


def kernel(
    q_hbm, bk_hbm, bv_hbm, pk_hbm, pv_hbm, go_hbm, len_ref, pfx_ref, cnt_ref,
    dq_hbm, dbk_hbm, dbv_hbm, dpk_ref,
    bk_ref, bv_ref, pk_ref, pv_ref, go_s, qb, wb, w_send, kbr, vbr, id_own, id_in, id_s,
    pack, g1, pick, ksel, s_s, p_s, ds_s, top_s, inv_s, pb_s, dk_s, dv_s, dq_s, dbk_s, dbv_s,
    dkb, r1, part_s, s2, r2, s3, r3,
    send_sem, recv_sem, local_sem,
):
    at = place()
    core = at["core"]
    other = 1 - core
    counter = [0]
    started = []

    def send(src, dst, to):
        k = counter[0]
        counter[0] += 1
        copy = pltpu.make_async_remote_copy(
            src_ref=src, dst_ref=dst, send_sem=send_sem.at[k], recv_sem=recv_sem.at[k],
            device_id=to, device_id_type=MESH,
        )
        copy.start()
        started.append(copy)
        return copy

    def cols(start, size):
        return pl.ds(pl.multiple_of(start, 128), size)

    barrier = pltpu.get_barrier_semaphore()
    partners = [peer(at, None, 0, 1)]
    partners += [peer(at, a, d, o) for a in "xyz" for d in (1, 2, 3) for o in (0, 1)]
    for to in partners:
        pl.semaphore_signal(barrier, inc=1, device_id=to, device_id_type=MESH)

    loads = [
        pltpu.make_async_copy(src, dst, local_sem.at[7 + n])
        for n, (src, dst) in enumerate(
            (
                (pk_hbm, pk_ref),
                (pv_hbm, pv_ref),
                (bk_hbm, bk_ref),
                (bv_hbm, bv_ref),
                (go_hbm, go_s),
                (q_hbm.at[:, cols(core * 2048, 2048)], qb.at[0]),
            )
        )
    ]
    for copy in loads:
        copy.start()
    id_tile = jnp.full((8, 128), pfx_ref[0], jnp.int32)
    id_own[...] = id_tile
    id_in[core] = id_tile
    loads[0].wait()
    loads[1].wait()
    for half in range(2):
        for head in range(4):
            rows, c128 = slice(half * 32, half * 32 + 32), slice(head * 128, head * 128 + 128)
            pack[half, head, 0] = pk_ref[rows, c128]
            pack[half, head, 1] = pv_ref[rows, c128]
    pl.semaphore_wait(barrier, len(partners))

    def grid(h, first):
        return (at[first], at["x"]) if h == 0 else (at["x"], at[first])

    first_copies = {}
    for h in range(HEADS):
        for half, (first, _) in enumerate(HALVES):
            here = (half, h, slice(None)) + grid(h, first) + (core,)
            first_copies[h, half] = []
            for d in range(4):
                for o in (0, 1):
                    if d == 0 and o == 0:
                        continue
                    to_core = other if o else core
                    axis = ("x" if h == 0 else first) if d else None
                    first_copies[h, half].append(
                        send(pack.at[half, 2 * to_core + h], g1.at[here], peer(at, axis, d, o))
                    )
            g1[here] = pack[half, 2 * core + h]

    def id_slot(half, d, c):
        return c if d == 0 else 2 + half * 6 + (d - 1) * 2 + c

    id_copies = [send(id_own, id_in.at[core], peer(at, None, 0, 1))]
    for half, (_, last) in enumerate(HALVES):
        for d in (1, 2, 3):
            for o in (0, 1):
                id_copies.append(send(id_own, id_in.at[id_slot(half, d, core)], peer(at, last, 4 - d, o)))

    pair = peer(at, None, 0, 1)
    loads[2].wait()
    loads[3].wait()
    pair_copies = [
        send(q_hbm.at[:, cols(other * 2048, 2048)], qb.at[1], pair),
        send(bk_ref.at[:, cols(other * 256, 256)], kbr.at[1], pair),
        send(bv_ref.at[:, cols(other * 256, 256)], vbr.at[1], pair),
    ]
    kbr[0] = bk_ref[:, cols(core * 256, 256)]
    vbr[0] = bv_ref[:, cols(core * 256, 256)]
    loads[4].wait()
    weight = lax.rsqrt(jnp.full((128, 128), cnt_ref[0], jnp.int32).astype(f32))
    live = lax.broadcasted_iota(jnp.int32, (128, 128), 0) < len_ref[0]
    weight = jnp.where(live, weight, 0.0)

    def weigh(i, _):
        theirs = go_s[:, cols(other * 2048 + i * 128, 128)].astype(f32) * weight
        w_send[:, cols(i * 128, 128)] = theirs.astype(bf16)
        ours = go_s[:, cols(core * 2048 + i * 128, 128)].astype(f32) * weight
        wb[0, :, cols(i * 128, 128)] = ours.astype(bf16)
        return 0

    lax.fori_loop(0, 16, weigh, 0)
    pair_copies.append(send(w_send, wb.at[1], pair))

    second_copies = {}
    for h in range(HEADS):
        for half in range(2):
            for copy in first_copies[h, half]:
                copy.wait_recv()
        for kv in range(KV):
            for half, (first, _) in enumerate(HALVES):
                axis = first if h == 0 else "x"
                block = g1.at[half, h, kv, at[axis]]
                second_copies[h, kv, half] = [send(block, block, peer(at, axis, d)) for d in (1, 2, 3)]

    for copy in id_copies:
        copy.wait_recv()
    id_copy = pltpu.make_async_copy(id_in.at[:, pl.ds(0, 1)], id_s, local_sem.at[2])
    id_copy.start()
    id_copy.wait()

    def prefix_of(half, d, b):
        return id_s[id_slot(half, d, other if b else core), 0, 0]

    last_copies = {}

    def last_step(h, kv, half, b):
        last = HALVES[half][1]
        for d in (1, 2, 3, 0):
            p = prefix_of(half, d, b)
            for xh in range(2):
                of = []
                for k in range(4):
                    x = xh * 2 + k // 2
                    rows = g1[half, h, kv, :, x, k % 2] if h == 0 else g1[half, h, kv, x, :, k % 2]
                    of.append(rows.reshape(128, 128))
                low = jnp.where(p == 0, of[0], of[1])
                rows = jnp.where(p < 2, low, jnp.where(p == 2, of[2], of[3]))
                if d:
                    pick[half, h, kv, d - 1, b, xh * 128:xh * 128 + 128] = rows
                else:
                    ksel[h, kv, b, half, 0, xh * 128:xh * 128 + 128] = rows
            if d:
                last_copies[h, kv, b, half, d] = send(
                    pick.at[half, h, kv, d - 1, b], ksel.at[h, kv, b, half, d], peer(at, last, d)
                )

    for h in range(HEADS):
        for b in (1, 0):
            for kv in range(KV):
                for half in range(2):
                    if b == 1:
                        for copy in second_copies[h, kv, half]:
                            copy.wait_recv()
                    last_step(h, kv, half, b)

    loads[5].wait()
    for copy in pair_copies:
        copy.wait_recv()

    spans = [(i, i * 256, 128 if i == 8 else 256) for i in (8, 0, 4, 1, 5, 2, 6, 3, 7)]

    def keys(kv, h, b, i):
        if i == 8:
            return (kbr, vbr)[kv][b, :, h * 128:h * 128 + 128]
        return ksel[h, kv, b, i // 4, i % 4]

    def rows_of(ref, t):
        h, b, j = t
        c = h * 1024 + j * 256
        return jnp.concatenate([ref[b, :, c:c + 128], ref[b, :, c + 128:c + 256]], 0)

    def split_query(t):
        query = rows_of(qb, t).astype(f32) * EXP2_SCALE
        high = query.astype(bf16)
        return jnp.concatenate([high, (query - high.astype(f32)).astype(bf16)], 1)

    def scores(t, slot, i, o, n, query, weighted):
        h, b, j = t
        if j == 0 and i < 8 and i % 4:
            last_copies[h, 0, b, i // 4, i % 4].wait_recv()
            last_copies[h, 1, b, i // 4, i % 4].wait_recv()
        k = keys(0, h, b, i)
        s = dot(query, jnp.concatenate([k, k], 1), 1, 1)
        if i == 8:
            row = lax.broadcasted_iota(jnp.int32, (256, 128), 0) % 128
            s = jnp.where(lax.broadcasted_iota(jnp.int32, (256, 128), 1) <= row, s, NEG)
        s_s[slot, :, o:o + n] = s
        top = s[:, :128] if n == 128 else jnp.maximum(s[:, :128], s[:, 128:])
        top_s[slot] = top if i == 8 else jnp.maximum(top_s[slot], top)
        p_s[slot, :, o:o + n] = dot(weighted, keys(1, h, b, i), 1, 1)

    def ds_slot(now):
        return now % 2 if now < 12 else now - 10

    def softmax(slot, keep, g):
        rows = slice(g * 32, g * 32 + 32)
        top = jnp.broadcast_to(jnp.max(top_s[slot, rows], axis=1, keepdims=True), (32, 128))
        total = mixed = None
        for o in range(0, 2176, 128):
            e = jnp.exp2(s_s[slot, rows, o:o + 128] - top)
            s_s[slot, rows, o:o + 128] = e
            ed = e * p_s[slot, rows, o:o + 128]
            total = e if total is None else total + e
            mixed = ed if mixed is None else mixed + ed
        inverse = 1.0 / jnp.sum(total, axis=1, keepdims=True)
        delta = jnp.broadcast_to(jnp.sum(mixed, axis=1, keepdims=True) * inverse, (32, 128))
        inv_s[keep, rows] = jnp.broadcast_to(inverse, (32, 128))
        for o in range(0, 2176, 128):
            e = s_s[slot, rows, o:o + 128]
            ds_s[keep, rows, o:o + 128] = (e * (p_s[slot, rows, o:o + 128] - delta)).astype(bf16)
            if o == 2048:
                pb_s[slot, rows] = (e * inverse).astype(bf16)

    def grad_query(t, keep):
        h, b, j = t
        dq = dot(ds_s[keep, :, :2048], ksel[h, 0, b].reshape(2048, 128), 1, 0)
        dq = dq + dot(ds_s[keep, :, 2048:], keys(0, h, b, 8), 1, 0)
        dq = (dq * (inv_s[keep] * SCALE)).astype(bf16)
        c = h * 1024 + j * 256
        dq_s[b, :, c:c + 128] = dq[:128]
        dq_s[b, :, c + 128:c + 256] = dq[128:]

    def local_values(t, slot, keep):
        dv = dot(pb_s[slot], rows_of(wb, t), 0, 0)
        dv_s[...] = dv if t[2] == 0 else dv_s[...] + dv
        return (rows_of(qb, t).astype(f32) * (inv_s[keep] * SCALE)).astype(bf16)

    def key_terms(t, slot, o, n, query):
        dk = dot(query, ds_s[slot, :, o:o + n], 0, 0)
        dk_s[:, o:o + n] = dk if t[2] == 0 else dk_s[:, o:o + n] + dk

    def finish_unit(h, b):
        local = slice(h * 128, h * 128 + 128)
        dbk_s[b, :, local] = dk_s[:, 2048:].T.astype(bf16)
        dbv_s[b, :, local] = dv_s[...].astype(bf16)
        for i in range(16):
            rows = slice(i % 2 * 128, i % 2 * 128 + 128)
            dkb[h, b, i // 8, i // 2 % 4, rows] = dk_s[:, i * 128:i * 128 + 128].T.astype(bf16)

    steps = [(h, b, j) for h in range(HEADS) for b in (1, 0) for j in range(4)]

    def pipeline(now):
        slot, before = now % 2, (now + 1) % 2
        ahead = steps[now] if now < 16 else None
        middle = steps[now - 1] if 0 < now <= 16 else None
        behind = steps[now - 2] if now >= 2 else None
        if ahead:
            query, weighted = split_query(ahead), rows_of(wb, ahead)
        if behind:
            keep = ds_slot(now - 2)
            scaled = local_values(behind, slot, keep)
            if now - 2 < 12:
                grad_query(behind, keep)
        for x, (i, o, n) in enumerate(spans):
            if ahead:
                scores(ahead, slot, i, o, n, query, weighted)
            if middle and x < 8:
                softmax(before, ds_slot(now - 1), x)
            if behind:
                key_terms(behind, keep, o, n, scaled)
        if behind and behind[2] == 3:
            finish_unit(behind[0], behind[1])

    def sum_last_send(h, b):
        copies = []
        for half, (_, last) in enumerate(HALVES):
            for d in (1, 2, 3):
                copies.append(
                    send(
                        dkb.at[h, b, half, d],
                        r1.at[h, half, d - 1, b],
                        peer(at, last, 4 - d),
                    )
                )
        return copies

    def sum_last(h, copies, terms, more, done):
        for copy in copies:
            copy.wait_recv()
        for half in range(2):
            ids = {(d, b): prefix_of(half, d, b) for d, b in terms}

            def block(i, _):
                rows = pl.ds(pl.multiple_of(i * 32, 32), 32)
                sums = [part_s[half, i, p] if more else jnp.zeros((32, 128), f32) for p in range(4)]
                for d, b in terms:
                    term = r1[h, half, d - 1, b, rows, :] if d else dkb[h, b, half, 0, rows, :]
                    term = term.astype(f32)
                    for p in range(4):
                        sums[p] = sums[p] + jnp.where(ids[d, b] == p, term, 0.0)
                for p in range(4):
                    if done:
                        s2[h, half, i % 4, (i // 4) * 2 + p // 2, p % 2] = sums[p].astype(bf16)
                    else:
                        part_s[half, i, p] = sums[p]
                return 0

            lax.fori_loop(0, 8, block, 0)

    early = [(d, 1) for d in range(4)] + [(0, 0)]
    late = [(d, 0) for d in (1, 2, 3)]

    def sum_first_send(h):
        return [
            send(s2.at[h, half, (at[first] + d) % 4], r2.at[h, half, d - 1], peer(at, first, d))
            for half, (first, _) in enumerate(HALVES)
            for d in (1, 2, 3)
        ]

    def sum_first(h, copies):
        for copy in copies:
            copy.wait_recv()
        for half, (first, _) in enumerate(HALVES):
            for x in range(4):
                total = s2[h, half, at[first], x].astype(f32)
                for d in range(3):
                    total = total + r2[h, half, d, x].astype(f32)
                s3[h, half, x] = total.astype(bf16)

    def sum_x_send(h):
        copies = []
        for half in range(2):
            for d in range(4):
                for o in (0, 1):
                    if d == 0 and o == 0:
                        continue
                    to_core = other if o else core
                    copies.append(
                        send(
                            s3.at[h, half, (at["x"] + d) % 4, to_core],
                            r3.at[h, half, d, o],
                            peer(at, "x" if d else None, d, o),
                        )
                    )
        return copies

    def sum_x(h, copies):
        for copy in copies:
            copy.wait_recv()
        for half in range(2):
            for o in (0, 1):
                total = (r3[h, half, 0, 1] if o else s3[h, half, at["x"], core]).astype(f32)
                for d in (1, 2, 3):
                    total = total + r3[h, half, d, o].astype(f32)
                head = 2 * (other if o else core) + h
                dpk_ref[half * 32:half * 32 + 32, cols(head * 128, 128)] = total.astype(bf16)

    local_copies = []

    def give_back(h, b, n):
        heads = cols(core * 2048 + h * 1024, 1024)
        src, dst = dq_s.at[b, :, h * 1024:h * 1024 + 1024], dq_hbm.at[:, heads]
        if b:
            return [send(src, dst, pair)]
        copy = pltpu.make_async_copy(src, dst, local_sem.at[n])
        copy.start()
        local_copies.append(copy)
        return []

    returned = []
    last_sums = {}
    mine = cols(core * 256, 256)
    for now in range(18):
        pipeline(now)
        if now in (5, 9, 13, 17):
            h, b, _ = steps[now - 2]
            last_sums[h, b] = sum_last_send(h, b)
            if now < 17:
                returned += give_back(h, b, 3 + h)
        if now == 13:
            returned.append(send(dbk_s.at[1], dbk_hbm.at[:, mine], pair))
            returned.append(send(dbv_s.at[1], dbv_hbm.at[:, mine], pair))
        if now == 14:
            sum_last(0, last_sums[0, 1] + last_sums[0, 0], early + late, False, True)
            first0 = sum_first_send(0)
    for n, (src, dst) in enumerate(((dbk_s, dbk_hbm), (dbv_s, dbv_hbm))):
        copy = pltpu.make_async_copy(src.at[0], dst.at[:, mine], local_sem.at[5 + n])
        copy.start()
        local_copies.append(copy)
    sum_last(1, last_sums[1, 1], early, False, False)
    for now in range(12, 16):
        grad_query(steps[now], ds_slot(now))
    give_back(1, 0, 4)
    sum_first(0, first0)
    x0 = sum_x_send(0)
    sum_last(1, last_sums[1, 0], late, True, True)
    first1 = sum_first_send(1)
    sum_x(0, x0)
    sum_first(1, first1)
    x1 = sum_x_send(1)
    sum_x(1, x1)

    for copy in returned:
        copy.wait_recv()
    for copy in local_copies:
        copy.wait()
    for copy in started:
        copy.wait_send()


COPIES = 13 + 28 + 4 + 24 + 48 + 24 + 12 + 28 + 4
ANY = pl.BlockSpec(memory_space=pl.ANY)
VMEM = pl.BlockSpec(memory_space=pltpu.VMEM)
SMEM = pl.BlockSpec(memory_space=pltpu.SMEM)


def place_results(dq, dbk, dbv, dpk, dq_out, dbk_out, dbv_out, dpk_out, dq_s, dbk_s, dbv_s, dpk_s, sem):
    parts = [(dq.at[pl.ds(i * 32, 32)], dq_s.at[pl.ds(i * 32, 32)], dq_out.at[pl.ds(i * 32, 32)]) for i in range(4)]
    parts += [(dbk, dbk_s, dbk_out), (dbv, dbv_s, dbv_out), (dpk, dpk_s, dpk_out)]
    reads = [pltpu.make_async_copy(a, b, sem.at[0, n]) for n, (a, b, _) in enumerate(parts)]
    writes = [pltpu.make_async_copy(b, c, sem.at[1, n]) for n, (_, b, c) in enumerate(parts)]
    for copy in reads:
        copy.start()
    for read, write in zip(reads, writes):
        read.wait()
        write.start()
    for copy in writes:
        copy.wait()


def on_device(bq, bk, bv, pk, pv, go, length, prefix, count):
    v = pltpu.VMEM
    outs = pl.pallas_call(
        kernel,
        out_shape=(
            jax.ShapeDtypeStruct((128, 4096), bf16),
            jax.ShapeDtypeStruct((128, 512), bf16),
            jax.ShapeDtypeStruct((128, 512), bf16),
            jax.ShapeDtypeStruct((64, 512), bf16),
        ),
        in_specs=[ANY] * 6 + [SMEM] * 3,
        out_specs=(ANY, ANY, ANY, VMEM),
        scratch_shapes=[
            v((128, 512), bf16),
            v((128, 512), bf16),
            v((64, 512), bf16),
            v((64, 512), bf16),
            v((128, 4096), bf16),
            v((2, 128, 2048), bf16),
            v((2, 128, 2048), bf16),
            v((128, 2048), bf16),
            v((2, 128, 256), bf16),
            v((2, 128, 256), bf16),
            v((8, 128), jnp.int32),
            v((14, 8, 128), jnp.int32),
            pltpu.SMEM((14, 1, 128), jnp.int32),
            v((2, 4, 2, 32, 128), bf16),
            v((2, 2, 2, 4, 4, 2, 32, 128), bf16),
            v((2, 2, 2, 3, 2, 256, 128), bf16),
            v((2, 2, 2, 2, 4, 256, 128), bf16),
            v((2, 256, 2176), f32),
            v((2, 256, 2176), f32),
            v((6, 256, 2176), bf16),
            v((2, 256, 128), f32),
            v((6, 256, 128), f32),
            v((2, 256, 128), bf16),
            v((128, 2176), f32),
            v((128, 128), f32),
            v((2, 128, 2048), bf16),
            v((2, 128, 256), bf16),
            v((2, 128, 256), bf16),
            v((2, 2, 2, 4, 256, 128), bf16),
            v((2, 2, 3, 2, 256, 128), bf16),
            v((2, 8, 4, 32, 128), f32),
            v((2, 2, 4, 4, 2, 32, 128), bf16),
            v((2, 2, 3, 4, 2, 32, 128), bf16),
            v((2, 2, 4, 2, 32, 128), bf16),
            v((2, 2, 4, 2, 32, 128), bf16),
            pltpu.SemaphoreType.DMA((COPIES,)),
            pltpu.SemaphoreType.DMA((COPIES,)),
            pltpu.SemaphoreType.DMA((13,)),
        ],
        compiler_params=pltpu.CompilerParams(
            collective_id=0, has_side_effects=True, vmem_limit_bytes=56 * 1024 * 1024
        ),
        cost_estimate=pl.CostEstimate(flops=10**10, bytes_accessed=10**7, transcendentals=10**7),
    )(bq[0], bk[0], bv[0], pk, pv, go[0], length, prefix, count)
    outs = pl.pallas_call(
        place_results,
        out_shape=tuple(jax.ShapeDtypeStruct(o.shape, o.dtype) for o in outs),
        in_specs=[ANY] * 4,
        out_specs=(ANY,) * 4,
        scratch_shapes=[v(o.shape, o.dtype) for o in outs] + [pltpu.SemaphoreType.DMA((2, 7))],
    )(*outs)
    return outs[0][None], outs[1][None], outs[2][None], outs[3]


def solution(mesh):
    both = ("grp", "seq")
    rows3, rows2, rows1 = P(both, None, None), P(both, None), P(both)
    return jax.shard_map(
        on_device,
        mesh=mesh,
        in_specs=(rows3, rows3, rows3, rows2, rows2, rows3, rows1, rows1, rows1),
        out_specs=(rows3, rows3, rows3, rows2),
        check_vma=False,
    )
```

profile of v0, /device:TPU:1, one launch (start us, length us, event | category | flops | bytes accessed | tf_op | source)
XLA Modules:
  0.0 82.3 jit_solution(5351902081853693624)
XLA Ops:
  2.6 77.4 %shard_map.120 = (bf16[128,4096]{1,0:T(8,128)(2,1)}, bf16[128,512]{1,0:T(8,128)(2,1)}, bf16[128,512]{1,0:T(8,128)(2,1)}, bf16[64,512]{1,0:T(8,128)(2,1)}) custom-call(bf16[128,4096]{1,0:T(8,128)(2,1)} %bitcast.7, bf16[128,512]{1,0:T(8,128)(2,1)} %bitcast.10, bf16[128,512]{1,0:T(8,128)(2,1)} %bitcast.11, bf16[64,512]{1,0:T(8,128)(2,1)} %pk_hbm.1, ...), custom_call_target="tpu_custom_call" | custom-call | flops 10000000000 | bytes 10000000 | tf_op jit(solution)/shard_map/pallas_call | solution.py:475
  80.0 2.1 %shard_map.121 = (bf16[128,4096]{1,0:T(8,128)(2,1)}, bf16[128,512]{1,0:T(8,128)(2,1)}, bf16[128,512]{1,0:T(8,128)(2,1)}, bf16[64,512]{1,0:T(8,128)(2,1)}) custom-call(bf16[128,4096]{1,0:T(8,128)(2,1)} %get-tuple-element.12.dq, bf16[128,512]{1,0:T(8,128)(2,1)} %get-tuple-element.13.dbk, bf16[128,512]{1,0:T(8,128)(2,1)} %get-tuple-element.14.dbv, ...), custom_call_target="tpu_custom_call" | custom-call | tf_op jit(solution)/shard_map/pallas_call | solution.py:530
where the time goes:
time: 82.5 us; the launch traced here: 82.3 us
  Pallas kernels  79.5 us (96%)
  between operations  2.76 us (3%)
    pallas_call x1, Pallas kernels, on_device(): pl.pallas_call(kernel, out_shape=(jax.ShapeDtypeStruct((128, 4096), bf16)...  77.4 us
    pallas_call x1, Pallas kernels, on_device(): pl.pallas_call(place_results, out_shape=tuple((jax.ShapeDtypeStruct(o.sha...  2.13 us

commit v1 on v0

--- a/solution.py
+++ b/solution.py
@@ -138,21 +138,6 @@
     ]
     kbr[0] = bk_ref[:, cols(core * 256, 256)]
     vbr[0] = bv_ref[:, cols(core * 256, 256)]
-    loads[4].wait()
-    weight = lax.rsqrt(jnp.full((128, 128), cnt_ref[0], jnp.int32).astype(f32))
-    live = lax.broadcasted_iota(jnp.int32, (128, 128), 0) < len_ref[0]
-    weight = jnp.where(live, weight, 0.0)
-
-    def weigh(i, _):
-        theirs = go_s[:, cols(other * 2048 + i * 128, 128)].astype(f32) * weight
-        w_send[:, cols(i * 128, 128)] = theirs.astype(bf16)
-        ours = go_s[:, cols(core * 2048 + i * 128, 128)].astype(f32) * weight
-        wb[0, :, cols(i * 128, 128)] = ours.astype(bf16)
-        return 0
-
-    lax.fori_loop(0, 16, weigh, 0)
-    pair_copies.append(send(w_send, wb.at[1], pair))
-
     second_copies = {}
     for h in range(HEADS):
         for half in range(2):
@@ -163,6 +148,21 @@
                 axis = first if h == 0 else "x"
                 block = g1.at[half, h, kv, at[axis]]
                 second_copies[h, kv, half] = [send(block, block, peer(at, axis, d)) for d in (1, 2, 3)]
+
+    loads[4].wait()
+    weight = lax.rsqrt(jnp.full((128, 128), cnt_ref[0], jnp.int32).astype(f32))
+    live = lax.broadcasted_iota(jnp.int32, (128, 128), 0) < len_ref[0]
+    weight = jnp.where(live, weight, 0.0)
+
+    def weigh(i, _):
+        theirs = go_s[:, cols(other * 2048 + i * 128, 128)].astype(f32) * weight
+        w_send[:, cols(i * 128, 128)] = theirs.astype(bf16)
+        ours = go_s[:, cols(core * 2048 + i * 128, 128)].astype(f32) * weight
+        wb[0, :, cols(i * 128, 128)] = ours.astype(bf16)
+        return 0
+
+    lax.fori_loop(0, 16, weigh, 0)
+    pair_copies.append(send(w_send, wb.at[1], pair))
 
     for copy in id_copies:
         copy.wait_recv()
@@ -314,88 +314,80 @@
             finish_unit(behind[0], behind[1])
 
     def sum_last_send(h, b):
+        return [
+            [
+                send(dkb.at[h, b, half, d], r1.at[h, half, d - 1, b], peer(at, last, 4 - d))
+                for d in (2, 1, 3)
+            ]
+            for half, (_, last) in enumerate(HALVES)
+        ]
+
+    def sum_last(h, half, copies, terms, more, done):
+        for copy in copies:
+            copy.wait_recv()
+        ids = {(d, b): prefix_of(half, d, b) for d, b in terms}
+
+        def block(i, _):
+            rows = pl.ds(pl.multiple_of(i * 32, 32), 32)
+            sums = [part_s[half, i, p] if more else jnp.zeros((32, 128), f32) for p in range(4)]
+            for d, b in terms:
+                term = r1[h, half, d - 1, b, rows, :] if d else dkb[h, b, half, 0, rows, :]
+                term = term.astype(f32)
+                for p in range(4):
+                    sums[p] = sums[p] + jnp.where(ids[d, b] == p, term, 0.0)
+            for p in range(4):
+                if done:
+                    s2[h, half, i % 4, (i // 4) * 2 + p // 2, p % 2] = sums[p].astype(bf16)
+                else:
+                    part_s[half, i, p] = sums[p]
+            return 0
+
+        lax.fori_loop(0, 8, block, 0)
+
+    early = [(d, 1) for d in range(4)] + [(0, 0)]
+    late = [(d, 0) for d in (1, 2, 3)]
+
+    def sum_first_send(h, half):
+        first = HALVES[half][0]
+        return [
+            send(s2.at[h, half, (at[first] + d) % 4], r2.at[h, half, d - 1], peer(at, first, d))
+            for d in (2, 1, 3)
+        ]
+
+    def sum_first(h, half, copies):
+        for copy in copies:
+            copy.wait_recv()
+        for x in range(4):
+            total = s2[h, half, at[HALVES[half][0]], x].astype(f32)
+            for d in range(3):
+                total = total + r2[h, half, d, x].astype(f32)
+            s3[h, half, x] = total.astype(bf16)
+
+    def sum_x_send(h, half):
         copies = []
-        for half, (_, last) in enumerate(HALVES):
-            for d in (1, 2, 3):
+        for d in (2, 1, 3, 0):
+            for o in (1, 0):
+                if d == 0 and o == 0:
+                    continue
+                to_core = other if o else core
                 copies.append(
                     send(
-                        dkb.at[h, b, half, d],
-                        r1.at[h, half, d - 1, b],
-                        peer(at, last, 4 - d),
+                        s3.at[h, half, (at["x"] + d) % 4, to_core],
+                        r3.at[h, half, d, o],
+                        peer(at, "x" if d else None, d, o),
                     )
                 )
         return copies
 
-    def sum_last(h, copies, terms, more, done):
+    def sum_x(h, half, copies):
         for copy in copies:
             copy.wait_recv()
-        for half in range(2):
-            ids = {(d, b): prefix_of(half, d, b) for d, b in terms}
-
-            def block(i, _):
-                rows = pl.ds(pl.multiple_of(i * 32, 32), 32)
-                sums = [part_s[half, i, p] if more else jnp.zeros((32, 128), f32) for p in range(4)]
-                for d, b in terms:
-                    term = r1[h, half, d - 1, b, rows, :] if d else dkb[h, b, half, 0, rows, :]
-                    term = term.astype(f32)
-                    for p in range(4):
-                        sums[p] = sums[p] + jnp.where(ids[d, b] == p, term, 0.0)
-                for p in range(4):
-                    if done:
-                        s2[h, half, i % 4, (i // 4) * 2 + p // 2, p % 2] = sums[p].astype(bf16)
-                    else:
-                        part_s[half, i, p] = sums[p]
-                return 0
-
-            lax.fori_loop(0, 8, block, 0)
-
-    early = [(d, 1) for d in range(4)] + [(0, 0)]
-    late = [(d, 0) for d in (1, 2, 3)]
-
-    def sum_first_send(h):
-        return [
-            send(s2.at[h, half, (at[first] + d) % 4], r2.at[h, half, d - 1], peer(at, first, d))
-            for half, (first, _) in enumerate(HALVES)
-            for d in (1, 2, 3)
-        ]
-
-    def sum_first(h, copies):
-        for copy in copies:
-            copy.wait_recv()
-        for half, (first, _) in enumerate(HALVES):
-            for x in range(4):
-                total = s2[h, half, at[first], x].astype(f32)
-                for d in range(3):
-                    total = total + r2[h, half, d, x].astype(f32)
-                s3[h, half, x] = total.astype(bf16)
-
-    def sum_x_send(h):
-        copies = []
-        for half in range(2):
-            for d in range(4):
-                for o in (0, 1):
-                    if d == 0 and o == 0:
-                        continue
-                    to_core = other if o else core
-                    copies.append(
-                        send(
-                            s3.at[h, half, (at["x"] + d) % 4, to_core],
-                            r3.at[h, half, d, o],
-                            peer(at, "x" if d else None, d, o),
-                        )
-                    )
-        return copies
-
-    def sum_x(h, copies):
-        for copy in copies:
-            copy.wait_recv()
-        for half in range(2):
-            for o in (0, 1):
-                total = (r3[h, half, 0, 1] if o else s3[h, half, at["x"], core]).astype(f32)
-                for d in (1, 2, 3):
-                    total = total + r3[h, half, d, o].astype(f32)
-                head = 2 * (other if o else core) + h
-                dpk_ref[half * 32:half * 32 + 32, cols(head * 128, 128)] = total.astype(bf16)
+        for o in (0, 1):
+            total = (r3[h, half, 0, 1] if o else s3[h, half, at["x"], core]).astype(f32)
+            for d in (1, 2, 3):
+                total = total + r3[h, half, d, o].astype(f32)
+            head = 2 * (other if o else core) + h
+            dpk_ref[half * 32:half * 32 + 32, cols(head * 128, 128)] = total.astype(bf16)
 
     local_copies = []
 
@@ -423,24 +415,33 @@
             returned.append(send(dbk_s.at[1], dbk_hbm.at[:, mine], pair))
             returned.append(send(dbv_s.at[1], dbv_hbm.at[:, mine], pair))
         if now == 14:
-            sum_last(0, last_sums[0, 1] + last_sums[0, 0], early + late, False, True)
-            first0 = sum_first_send(0)
+            first0 = []
+            for half in range(2):
+                sum_last(0, half, last_sums[0, 1][half] + last_sums[0, 0][half], early + late, False, True)
+                first0.append(sum_first_send(0, half))
     for n, (src, dst) in enumerate(((dbk_s, dbk_hbm), (dbv_s, dbv_hbm))):
         copy = pltpu.make_async_copy(src.at[0], dst.at[:, mine], local_sem.at[5 + n])
         copy.start()
         local_copies.append(copy)
-    sum_last(1, last_sums[1, 1], early, False, False)
+    for half in range(2):
+        sum_last(1, half, last_sums[1, 1][half], early, False, False)
     for now in range(12, 16):
         grad_query(steps[now], ds_slot(now))
     give_back(1, 0, 4)
-    sum_first(0, first0)
-    x0 = sum_x_send(0)
-    sum_last(1, last_sums[1, 0], late, True, True)
-    first1 = sum_first_send(1)
-    sum_x(0, x0)
-    sum_first(1, first1)
-    x1 = sum_x_send(1)
-    sum_x(1, x1)
+    x0, first1, x1 = [], [], []
+    for half in range(2):
+        sum_first(0, half, first0[half])
+        x0.append(sum_x_send(0, half))
+    for half in range(2):
+        sum_last(1, half, last_sums[1, 0][half], late, True, True)
+        first1.append(sum_first_send(1, half))
+    for half in range(2):
+        sum_x(0, half, x0[half])
+    for half in range(2):
+        sum_first(1, half, first1[half])
+        x1.append(sum_x_send(1, half))
+    for half in range(2):
+        sum_x(1, half, x1[half])
 
     for copy in returned:
         copy.wait_recv()

time: 82.5 us -> 81.4 us (0.987)
  Pallas kernels: 79.5 us -> 78.5 us
    pallas_call x1, Pallas kernels: 77.4 us -> 76.3 us  [on_device(): pl.pallas_call(kernel, out_shape=(jax.ShapeDtypeStruct((128, 4096), bf16)...]
where the time goes in v1:
time: 81.4 us; the launch traced here: 81.2 us
  Pallas kernels  78.5 us (96%)
  between operations  2.76 us (3%)
    pallas_call x1, Pallas kernels, on_device(): pl.pallas_call(kernel, out_shape=(jax.ShapeDtypeStruct((128, 4096), bf16)...  76.3 us
    pallas_call x1, Pallas kernels, on_device(): pl.pallas_call(place_results, out_shape=tuple((jax.ShapeDtypeStruct(o.sha...  2.13 us

profile of v1, /device:TPU:1, one launch (start us, length us, event | category | flops | bytes accessed | tf_op | source)
XLA Modules:
  0.0 81.2 jit_solution(11667704793275482668)
XLA Ops:
  2.6 76.3 %shard_map.120 = (bf16[128,4096]{1,0:T(8,128)(2,1)}, bf16[128,512]{1,0:T(8,128)(2,1)}, bf16[128,512]{1,0:T(8,128)(2,1)}, bf16[64,512]{1,0:T(8,128)(2,1)}) custom-call(bf16[128,4096]{1,0:T(8,128)(2,1)} %bitcast.7, bf16[128,512]{1,0:T(8,128)(2,1)} %bitcast.10, bf16[128,512]{1,0:T(8,128)(2,1)} %bitcast.11, bf16[64,512]{1,0:T(8,128)(2,1)} %pk_hbm.1, ...), custom_call_target="tpu_custom_call" | custom-call | flops 10000000000 | bytes 10000000 | tf_op jit(solution)/shard_map/pallas_call | solution.py:476
  78.9 2.1 %shard_map.121 = (bf16[128,4096]{1,0:T(8,128)(2,1)}, bf16[128,512]{1,0:T(8,128)(2,1)}, bf16[128,512]{1,0:T(8,128)(2,1)}, bf16[64,512]{1,0:T(8,128)(2,1)}) custom-call(bf16[128,4096]{1,0:T(8,128)(2,1)} %get-tuple-element.12.dq, bf16[128,512]{1,0:T(8,128)(2,1)} %get-tuple-element.13.dbk, bf16[128,512]{1,0:T(8,128)(2,1)} %get-tuple-element.14.dbv, ...), custom_call_target="tpu_custom_call" | custom-call | tf_op jit(solution)/shard_map/pallas_call | solution.py:531
